TPU v7x, 128 devices: a whole 4x4x4 slice. The times are simulated.
128 devices in a mesh: view: 4 (over y), space: 32 (over x, z, core).
Axes of the slice: x: 4, y: 4, z: 4, core: 2. Of those that a mesh axis runs over, the one named last changes fastest.
Arguments:
- estimate: float32 [3072, 128, 128], P('space'), may hold values from 0.5 to 2
- view_data: float32 [4, 3072, 128, 128], P('view', 'space'), may hold values from 0.2 to 5
- blend_weights: float32 [4, 3072, 128, 128], P('view', 'space'), may hold values from 0.1 to 1
- kernels: float32 [4, 3, 31], P('view'), may hold values from 0.01 to 1.1
- shifts: int32 [4], P('view'), may hold values from 0 to 15, as said below
Outputs:
- updated: float32 [3072, 128, 128], P('space')
Inputs may be any that keep to these rules, and one draw needn't show every extreme that they name: `shifts`: some view's shift is exactly 15.
All inputs are finite; a program needn't handle non-finite values.
Results may differ from a plain program's by a relative error of at most 0.0001.
Values sent between devices are 32-bit elements; how exact they have to be, the bound alone decides.
No kernel may reach another device: no remote copies, remote signals or barrier semaphores. Data moves between devices by JAX's collectives and lax.ppermute only.
A program may use at most 128 MiB of HBM per device.

v0:
```python
import jax
import jax.numpy as jnp
from jax import lax
from jax.sharding import PartitionSpec as P

OFF = 16
ITERS = 2


background_level = 0.1


def extended_2(block, sides, width):
    for axis, dim in sides:
        count = lax.axis_size(axis)
        forward = [(i, i + 1) for i in range(count - 1)]
        backward = [(target, source) for source, target in forward]
        low = lax.ppermute(
            lax.slice_in_dim(block, block.shape[dim] - width, None, axis=dim), axis, forward
        )
        high = lax.ppermute(lax.slice_in_dim(block, 0, width, axis=dim), axis, backward)
        block = jnp.concatenate([low, block, high], axis=dim)
    return block


def shifted(value, axis, steps):
    count = lax.axis_size(axis)
    leading, last = (max(0, -steps), min(count, count - steps))
    return lax.ppermute(value, axis, [(source, source + steps) for source in range(leading, last)])


def band_matrix(kernel, row_count, col_count, lowest, flipped):
    tap_count = kernel.shape[0]
    offset_grid = jnp.arange(col_count)[None, :] - jnp.arange(row_count)[:, None] - lowest
    tap_index = offset_grid if flipped else tap_count - 1 - offset_grid
    matches = (tap_index[:, :, None] == jnp.arange(tap_count)[None, None, :]).astype(kernel.dtype)
    return jnp.sum(matches * kernel[None, None, :], axis=-1)


def transverse(volume, kernel_y, kernel_x, flipped):
    half_taps = (kernel_y.shape[0] - 1) // 2
    across_y = band_matrix(kernel_y, volume.shape[1], volume.shape[1], -half_taps, flipped)
    across_x = band_matrix(kernel_x, volume.shape[2], volume.shape[2], -half_taps, flipped)
    volume = jnp.einsum("ab,zbx->zax", across_y, volume, precision=lax.Precision.HIGHEST)
    return jnp.einsum("zyb,ab->zya", volume, across_x, precision=lax.Precision.HIGHEST)


def on_device(estimate, view_data, blend_weights, kernels, shifts):
    depth, row_count, col_count = estimate.shape
    tap_count = kernels.shape[2]
    half_taps = (tap_count - 1) // 2
    span = 2 * half_taps
    normalized = kernels[0] / jnp.sum(kernels[0], axis=1, keepdims=True)
    shift = shifts[0]
    along_conv = band_matrix(normalized[0], depth + span, depth + 2 * span, 0, False)
    along_corr = band_matrix(normalized[0], depth, depth + span, 0, True)
    data_padded = extended_2(view_data[0], (("space", 0),), half_taps)
    weights = blend_weights[0]
    weight_sum = lax.psum(weights, "view")
    rim_width = OFF + span - 1
    for iteration in range(ITERS):
        extended = extended_2(estimate, (("space", 0),), rim_width)
        anchor = shift + (rim_width - span)
        window = lax.dynamic_slice_in_dim(extended, anchor, depth + 2 * span, 0)
        blurred_z = jnp.einsum("ab,byx->ayx", along_conv, window, precision=lax.Precision.HIGHEST)
        blurred = transverse(blurred_z, normalized[1], normalized[2], False) + background_level
        quotient = data_padded / blurred
        returned_z = jnp.einsum(
            "ab,byx->ayx", along_corr, quotient, precision=lax.Precision.HIGHEST
        )
        returned = transverse(returned_z, normalized[1], normalized[2], True)
        spread = jnp.zeros((depth + OFF, row_count, col_count), jnp.float32)
        spread = lax.dynamic_update_slice_in_dim(spread, returned, shift, 0)
        incoming = shifted(spread[depth:], "space", 1)
        correction = spread[:depth].at[:OFF].add(incoming)
        weighted = weights * correction
        combined = lax.psum(weighted, "view")
        estimate = estimate * combined / weight_sum
    return estimate


def solution(mesh):
    return jax.shard_map(
        on_device,
        mesh=mesh,
        in_specs=(
            P("space", None, None),
            P("view", "space", None, None),
            P("view", "space", None, None),
            P("view", None, None),
            P("view"),
        ),
        out_specs=P("space", None, None),
        check_vma=False,
    )
```

profile of v0, /device:TPU:96, one launch (start us, length us, event | category | flops | bytes accessed | tf_op | source)
XLA Modules:
  0.0 688.6 jit_solution(3613880074868016226)
XLA Ops:
  6.5 6.0 fusion.53
  12.6 1.9 collective-permute-start.3
  14.5 2.4 collective-permute-start.2
  16.9 3.1 slice_bitcast_fusion.1
  20.0 5.1 collective-permute-start
  25.1 1.9 collective-permute-start.1
  27.7 0.1 reduce_sum.62
  27.8 0.1 bitcast_divide_fusion
  27.9 0.3 select_reduce_fusion.5
  28.2 0.4 select_reduce_fusion
  28.6 0.7 select_reduce_fusion.3
  29.3 18.1 %collective-permute-done.3 = f32[45,128,128]{2,1,0:T(8,128)S(1)} collective-permute-done((f32[45,128,128]{2,1,0:T(8,128)}, f32[45,128,128]{2,1,0:T(8,128)S(1)}, u32[]{:S(2)}, u32[]{:S(2)}) %collective-permute-start.3) | collective-permute-done | bytes 2949152 | tf_op jit(solution)/shard_map/ppermute | solution.py:21
  47.5 3.8 collective-permute-done.2
  51.3 5.7 fusion.7
  57.0 14.3 %fusion.2 = f32[126,128,128]{2,0,1:T(8,128)S(1)} fusion(f32[156,128,128]{2,1,0:T(8,128)S(1)} %fusion.7, f32[126,156]{0,1:T(8,128)S(1)} %select_reduce_fusion), kind=kOutput, calls=%fused_computation.8 | convolution fusion | flops 3864526848 | bytes 18559776 | tf_op jit(solution)/shard_map/ab,byx->ayx/dot_general | solution.py:65
  71.4 16.8 %fusion.18 = f32[126,128,128]{2,1,0:T(8,128)S(1)} fusion(f32[126,128,128]{2,0,1:T(8,128)S(1)} %fusion.2, f32[128,128]{1,0:T(8,128)S(1)} %get-tuple-element.32), kind=kOutput, calls=%fused_computation.25 | convolution fusion | flops 3170893824 | bytes 16580608 | tf_op jit(solution)/shard_map/ab,zbx->zax/dot_general | solution.py:44
  88.2 0.0 collective-permute-done
  88.2 0.0 collective-permute-done.1
  88.2 16.1 %add_divide_fusion.1 = f32[126,128,128]{2,1,0:T(8,128)S(1)} fusion(f32[15,128,128]{2,1,0:T(8,128)} %collective-permute-done.1, f32[96,128,128]{2,1,0:T(8,128)} %bitcast.77, f32[15,128,128]{2,1,0:T(8,128)} %collective-permute-done, f32[126,128,128]{2,1,0:T(8,128)S(1)} %fusion.18, f32[128,128]{1,0:T(8,128)S(1)} %get-tuple-element.31), kind=kOutput, calls=%fused_computation.28 | convolution fusion | flops 3179151360 | bytes 24838144 | tf_op jit(solution)/shard_map/zyb,ab->zya/dot_general | solution.py:45
  104.3 11.1 %fusion.10 = f32[96,128,128]{2,0,1:T(8,128)S(1)} fusion(f32[126,128,128]{2,1,0:T(8,128)S(1)} %add_divide_fusion.1, f32[96,126]{1,0:T(8,128)S(1)} %select_reduce_fusion.5), kind=kOutput, calls=%fused_computation.16 | convolution fusion | flops 2378170368 | bytes 14597376 | tf_op jit(solution)/shard_map/ab,byx->ayx/dot_general | solution.py:68
  115.4 10.2 %fusion.26 = f32[96,128,128]{1,2,0:T(8,128)S(1)} fusion(f32[96,128,128]{2,0,1:T(8,128)S(1)} %fusion.10, f32[128,128]{1,0:T(8,128)S(1)} %get-tuple-element.33), kind=kOutput, calls=%fused_computation.35 | convolution fusion | flops 2415919104 | bytes 12648448 | tf_op jit(solution)/shard_map/ab,zbx->zax/dot_general | solution.py:44
  125.6 0.9 broadcast.99.clone
  126.5 5.3 fusion.28
  131.8 0.1 slice.121
  131.9 3.3 collective-permute-start.4
  135.2 0.0 slice-start
  135.2 0.0 slice-start.1
  135.2 0.4 slice.119
  135.7 12.4 %collective-permute-done.4 = f32[16,128,128]{2,1,0:T(8,128)S(1)} collective-permute-done((f32[16,128,128]{2,1,0:T(8,128)S(1)}, f32[16,128,128]{2,1,0:T(8,128)S(1)}, u32[]{:S(2)}, u32[]{:S(2)}) %collective-permute-start.4) | collective-permute-done | bytes 1048608 | tf_op jit(solution)/shard_map/ppermute | solution.py:29
  148.0 0.1 fusion.39
  148.2 0.0 slice-done
  148.2 0.0 slice-done.1
  148.2 4.0 bitcast_multiply_fusion.1
  152.2 0.0 all-reduce.6.cloned.1.call-update
  152.2 0.0 all-reduce.4.cloned.1.call-start
  152.3 234.0 %all-reduce.6.cloned.1.call-done = (f32[96,128,128]{2,1,0:T(8,128)}, f32[96,128,128]{2,1,0:T(8,128)}) async-done(((f32[96,128,128]{2,1,0:T(8,128)}, f32[96,128,128]{2,1,0:T(8,128)}), (f32[96,128,128]{2,1,0:T(8,128)}, f32[96,128,128]{2,1,0:T(8,128)})) %all-reduce.6.cloned.1.call-update) | async-done | bytes 12582928 | tf_op jit(solution)/shard_map/psum | solution.py:59
  386.2 8.5 %multiply_divide_fusion.1 = f32[96,128,128]{2,1,0:T(8,128)S(1)} fusion(f32[96,128,128]{2,1,0:T(8,128)} %get-tuple-element.35, f32[96,128,128]{2,1,0:T(8,128)} %param.9, f32[96,128,128]{2,1,0:T(8,128)} %get-tuple-element.36), kind=kLoop, calls=%fused_computation.38 | loop fusion | flops 3145728 | bytes 25165824 | tf_op jit(solution)/shard_map/div | solution.py:78
  394.7 0.0 copy-start
  394.7 0.4 fusion.52
  395.1 2.1 collective-permute-start.6
  397.2 2.3 collective-permute-start.5
  399.5 30.4 %collective-permute-done.6 = f32[45,128,128]{2,1,0:T(8,128)S(1)} collective-permute-done((f32[45,128,128]{2,1,0:T(8,128)S(1)}, f32[45,128,128]{2,1,0:T(8,128)S(1)}, u32[]{:S(2)}, u32[]{:S(2)}) %collective-permute-start.6) | collective-permute-done | bytes 2949152 | tf_op jit(solution)/shard_map/ppermute | solution.py:21
  429.9 3.8 collective-permute-done.5
  433.7 4.3 fusion.5
  438.0 19.3 %fusion = f32[126,128,128]{2,0,1:T(8,128)} fusion(f32[156,128,128]{2,1,0:T(8,128)S(1)} %fusion.5, f32[126,156]{0,1:T(8,128)S(1)} %select_reduce_fusion), kind=kOutput, calls=%fused_computation.6 | convolution fusion | flops 3864526848 | bytes 18559776 | tf_op jit(solution)/shard_map/ab,byx->ayx/dot_general | solution.py:65
  457.3 17.5 %fusion.16 = f32[126,128,128]{2,1,0:T(8,128)S(1)} fusion(f32[126,128,128]{2,0,1:T(8,128)} %fusion, f32[128,128]{1,0:T(8,128)S(1)} %get-tuple-element.32), kind=kOutput, calls=%fused_computation.23 | convolution fusion | flops 3170893824 | bytes 16580608 | tf_op jit(solution)/shard_map/ab,zbx->zax/dot_general | solution.py:44
  474.8 16.1 %add_divide_fusion = f32[126,128,128]{2,1,0:T(8,128)S(1)} fusion(f32[15,128,128]{2,1,0:T(8,128)} %collective-permute-done.1, f32[96,128,128]{2,1,0:T(8,128)} %bitcast.78, f32[15,128,128]{2,1,0:T(8,128)} %collective-permute-done, f32[126,128,128]{2,1,0:T(8,128)S(1)} %fusion.16, f32[128,128]{1,0:T(8,128)S(1)} %get-tuple-element.31), kind=kOutput, calls=%fused_computation.27 | convolution fusion | flops 3179151360 | bytes 24838144 | tf_op jit(solution)/shard_map/zyb,ab->zya/dot_general | solution.py:45
  490.8 11.1 %fusion.8 = f32[96,128,128]{2,0,1:T(8,128)S(1)} fusion(f32[126,128,128]{2,1,0:T(8,128)S(1)} %add_divide_fusion, f32[96,126]{1,0:T(8,128)S(1)} %select_reduce_fusion.5), kind=kOutput, calls=%fused_computation.14 | convolution fusion | flops 2378170368 | bytes 14597376 | tf_op jit(solution)/shard_map/ab,byx->ayx/dot_general | solution.py:68
  502.0 10.0 %fusion.24 = f32[96,128,128]{1,2,0:T(8,128)S(1)} fusion(f32[96,128,128]{2,0,1:T(8,128)S(1)} %fusion.8, f32[128,128]{1,0:T(8,128)S(1)} %get-tuple-element.33), kind=kOutput, calls=%fused_computation.33 | convolution fusion | flops 2415919104 | bytes 12648448 | tf_op jit(solution)/shard_map/ab,zbx->zax/dot_general | solution.py:44
  512.0 0.9 broadcast.99
  512.9 5.3 fusion.31
  518.2 0.0 slice-start.2
  518.2 0.1 slice.126
  518.3 0.0 slice-start.3
  518.3 3.4 collective-permute-start.7
  521.7 0.4 slice.124
  522.2 12.5 %collective-permute-done.7 = f32[16,128,128]{2,1,0:T(8,128)S(1)} collective-permute-done((f32[16,128,128]{2,1,0:T(8,128)S(1)}, f32[16,128,128]{2,1,0:T(8,128)S(1)}, u32[]{:S(2)}, u32[]{:S(2)}) %collective-permute-start.7) | collective-permute-done | bytes 1048608 | tf_op jit(solution)/shard_map/ppermute | solution.py:29
  534.7 0.1 fusion.38
  534.8 0.0 slice-done.2
  534.8 0.0 slice-done.3
  534.8 3.9 bitcast_multiply_fusion
  538.7 0.0 all-reduce.4.cloned.1.call-update
  538.7 130.8 %all-reduce.4.cloned.1.call-done = f32[96,128,128]{2,1,0:T(8,128)} async-done(((f32[96,128,128]{2,1,0:T(8,128)}), f32[96,128,128]{2,1,0:T(8,128)}) %all-reduce.4.cloned.1.call-update) | async-done | bytes 6291472 | tf_op jit(solution)/shard_map/psum | solution.py:77
  669.5 11.9 %multiply_divide_fusion = f32[96,128,128]{2,1,0:T(8,128)} fusion(f32[96,128,128]{2,1,0:T(8,128)} %get-tuple-element.35, f32[96,128,128]{2,1,0:T(8,128)} %copy-done, f32[96,128,128]{2,1,0:T(8,128)} %all-reduce.4.cloned.1.call-done), kind=kLoop, calls=%fused_computation.37 | loop fusion | flops 3145728 | bytes 25165824 | tf_op jit(solution)/shard_map/div | solution.py:78
  (10 shorter events, 0.1 us)
Async XLA Ops:
  6.5 21.1 %copy-start.1 = (f32[1,3,31]{2,0,1:T(1,128)S(1)}, f32[1,3,31]{2,0,1:T(1,128)}, u32[]{:S(2)}) copy-start(f32[1,3,31]{2,0,1:T(1,128)} %param.12) | copy-start | bytes 1120
  6.5 379.7 %all-reduce.6.cloned.1.call-start = ((), (), s32[]{:S(2)}) async-start(), calls=%async_computation.1 | async-start | bytes 25165824 | tf_op jit(solution)/shard_map/psum | solution.py:59
  12.6 34.9 %collective-permute-start.3 = (f32[45,128,128]{2,1,0:T(8,128)}, f32[45,128,128]{2,1,0:T(8,128)S(1)}, u32[]{:S(2)}, u32[]{:S(2)}) collective-permute-start(f32[45,128,128]{2,1,0:T(8,128)} %get-tuple-element.39), channel_id=1, source_target_pairs={{1,0},{2,1},{3,2},{4,3},{5,4},{6,5},{7,6},{8,7},{9,8},{10,9},{11,1... | collective-permute-start | bytes 8847368 | tf_op jit(solution)/shard_map/ppermute | solution.py:21
  14.5 36.8 %collective-permute-start.2 = (f32[45,128,128]{2,1,0:T(8,128)}, f32[45,128,128]{2,1,0:T(8,128)}, u32[]{:S(2)}, u32[]{:S(2)}) collective-permute-start(f32[45,128,128]{2,1,0:T(8,128)} %get-tuple-element.40), channel_id=1, source_target_pairs={{0,1},{1,2},{2,3},{3,4},{4,5},{5,6},{6,7},{7,8},{8,9},{9,10},{10,1... | collective-permute-start | bytes 8847368 | tf_op jit(solution)/shard_map/ppermute | solution.py:18
  20.0 68.2 %collective-permute-start = (f32[15,128,128]{2,1,0:T(8,128)}, f32[15,128,128]{2,1,0:T(8,128)}, u32[]{:S(2)}, u32[]{:S(2)}) collective-permute-start(f32[15,128,128]{2,1,0:T(8,128)} %get-tuple-element.41), channel_id=1, source_target_pairs={{0,1},{1,2},{2,3},{3,4},{4,5},{5,6},{6,7},{7,8},{8,9},{9,10},{10,1... | collective-permute-start | bytes 2949128 | tf_op jit(solution)/shard_map/ppermute | solution.py:18
  25.1 63.1 %collective-permute-start.1 = (f32[15,128,128]{2,1,0:T(8,128)}, f32[15,128,128]{2,1,0:T(8,128)}, u32[]{:S(2)}, u32[]{:S(2)}) collective-permute-start(f32[15,128,128]{2,1,0:T(8,128)} %get-tuple-element.42), channel_id=1, source_target_pairs={{1,0},{2,1},{3,2},{4,3},{5,4},{6,5},{7,6},{8,7},{9,8},{10,9},{11,1... | collective-permute-start | bytes 2949128 | tf_op jit(solution)/shard_map/ppermute | solution.py:21
  131.9 16.1 %collective-permute-start.4 = (f32[16,128,128]{2,1,0:T(8,128)S(1)}, f32[16,128,128]{2,1,0:T(8,128)S(1)}, u32[]{:S(2)}, u32[]{:S(2)}) collective-permute-start(f32[16,128,128]{2,1,0:T(8,128)S(1)} %slice.121), channel_id=1, source_target_pairs={{0,1},{1,2},{2,3},{3,4},{4,5},{5,6},{6,7},{7,8},{8,9},{9,10},{10,1... | collective-permute-start | bytes 3145736 | tf_op jit(solution)/shard_map/ppermute | solution.py:29
  135.2 12.9 %slice-start = ((s8[6291456]{0:T(1024)(128)(4,1)}), s8[4194304]{0:T(1024)(128)(4,1)S(1)}, s32[]{:S(2)}) async-start(s8[6291456]{0:T(1024)(128)(4,1)} %bitcast.73), calls=%async_computation.2 | async-start | bytes 8388608
  135.2 12.9 %slice-start.1 = ((s8[6291456]{0:T(1024)(128)(4,1)}), s8[2097152]{0:T(1024)(128)(4,1)S(1)}, s32[]{:S(2)}) async-start(s8[6291456]{0:T(1024)(128)(4,1)} %bitcast.73), calls=%async_computation.3 | async-start | bytes 4194304
  152.2 517.3 %all-reduce.4.cloned.1.call-start = ((), (), s32[]{:S(2)}) async-start(), calls=%async_computation | async-start | bytes 12582912 | tf_op jit(solution)/shard_map/psum | solution.py:77
  394.7 43.2 %copy-start = (f32[96,128,128]{2,1,0:T(8,128)}, f32[96,128,128]{2,1,0:T(8,128)S(1)}, u32[]{:S(2)}) copy-start(f32[96,128,128]{2,1,0:T(8,128)S(1)} %multiply_divide_fusion.1) | copy-start | bytes 18874372
  395.1 34.7 %collective-permute-start.6 = (f32[45,128,128]{2,1,0:T(8,128)S(1)}, f32[45,128,128]{2,1,0:T(8,128)S(1)}, u32[]{:S(2)}, u32[]{:S(2)}) collective-permute-start(f32[45,128,128]{2,1,0:T(8,128)S(1)} %get-tuple-element.37), channel_id=1, source_target_pairs={{1,0},{2,1},{3,2},{4,3},{5,4},{6,5},{7,6},{8,7},{9,8},{10,9},{11,1... | collective-permute-start | bytes 8847368 | tf_op jit(solution)/shard_map/ppermute | solution.py:21
  397.2 36.5 %collective-permute-start.5 = (f32[45,128,128]{2,1,0:T(8,128)S(1)}, f32[45,128,128]{2,1,0:T(8,128)S(1)}, u32[]{:S(2)}, u32[]{:S(2)}) collective-permute-start(f32[45,128,128]{2,1,0:T(8,128)S(1)} %get-tuple-element.38), channel_id=1, source_target_pairs={{0,1},{1,2},{2,3},{3,4},{4,5},{5,6},{6,7},{7,8},{8,9},{9,10},{10,1... | collective-permute-start | bytes 8847368 | tf_op jit(solution)/shard_map/ppermute | solution.py:18
  518.2 16.6 %slice-start.2 = ((s8[6291456]{0:T(1024)(128)(4,1)}), s8[4194304]{0:T(1024)(128)(4,1)S(1)}, s32[]{:S(2)}) async-start(s8[6291456]{0:T(1024)(128)(4,1)} %bitcast.75), calls=%async_computation.4 | async-start | bytes 8388608
  518.3 16.5 %slice-start.3 = ((s8[6291456]{0:T(1024)(128)(4,1)}), s8[2097152]{0:T(1024)(128)(4,1)S(1)}, s32[]{:S(2)}) async-start(s8[6291456]{0:T(1024)(128)(4,1)} %bitcast.75), calls=%async_computation.5 | async-start | bytes 4194304
  518.3 16.4 %collective-permute-start.7 = (f32[16,128,128]{2,1,0:T(8,128)S(1)}, f32[16,128,128]{2,1,0:T(8,128)S(1)}, u32[]{:S(2)}, u32[]{:S(2)}) collective-permute-start(f32[16,128,128]{2,1,0:T(8,128)S(1)} %slice.126), channel_id=1, source_target_pairs={{0,1},{1,2},{2,3},{3,4},{4,5},{5,6},{6,7},{7,8},{8,9},{9,10},{10,1... | collective-permute-start | bytes 3145736 | tf_op jit(solution)/shard_map/ppermute | solution.py:29
Sparse Core Ops, SparseCore 0:
  152.3 233.8 all-reduce.5
  538.8 130.6 all-reduce.3
where the time goes:
time: 694 us; the launch traced here: 689 us
  waiting for transfers between devices  446 us (64%)
  matrix products  153 us (22%)
  other arithmetic  40.1 us (6%)
  starting transfers between devices  22.4 us (3%)
  between operations  14.7 us (2%)
  local copies, waits for them, and re-layouts  12.4 us (2%)
    psum x1, waiting for transfers between devices, on_device(): weight_sum = lax.psum(weights, 'view')  234 us
    psum x1, waiting for transfers between devices, on_device(): combined = lax.psum(weighted, 'view')  131 us
    dot_general x4, matrix products, transverse(): jnp.einsum('ab,zbx->zax', across_y, volume, precision=lax.Precision.HIGHEST)  54.5 us
    ppermute x3, waiting for transfers between devices, extended_2(): lax.ppermute(lax.slice_in_dim(block, 0, width, axis=dim), axis, backward)  48.5 us
    dot_general x4, matrix products, transverse(): jnp.einsum('zyb,ab->zya', volume, across_x, precision=lax.Precision.HIGHEST)  42.7 us
    dot_general x2, matrix products, on_device(): jnp.einsum('ab,byx->ayx', along_conv, window, precision=lax.Precision.HIG...  33.6 us
    ppermute x2, waiting for transfers between devices, shifted(): lax.ppermute(value, axis, [(source, source + steps) for source in range(l...  24.9 us
    dot_general x2, matrix products, on_device(): jnp.einsum('ab,byx->ayx', along_corr, quotient, precision=lax.Precision.H...  22.2 us
  transfers between devices with their start and end apart: 10, of which 8 were waited for; matrix products, arithmetic and copies ran while one was open for 6% of the time, Pallas kernels for 0%

commit v1 on v0

v1 whole, which is shorter than its diff:
```python
import functools

import jax
import jax.numpy as jnp
from jax import lax
from jax.experimental import pallas as pl
from jax.experimental.pallas import tpu as pltpu
from jax.sharding import PartitionSpec as P

F32, BF16 = jnp.float32, jnp.bfloat16
ITERS = 2
BACKGROUND = 0.1
BLOCK = 96
PLANE = 128
RIM = 32
VMEM = 50 << 20
EDGE, INNER = 16, 8
OPPOSITE, PLUS, MINUS, OWN = range(4)
STEP = (2, 1, 3, 0)


def halves(m):
    high = lax.reduce_precision(m, 8, 7)
    return high.astype(BF16), (m - high).astype(BF16)


def split(value):
    high = value.astype(BF16)
    return high, (value - high.astype(F32)).astype(BF16)


def band(taps, rows, cols, index):
    tap = index(jnp.arange(rows)[:, None], jnp.arange(cols)[None, :])
    return jnp.sum(jnp.where(tap[:, :, None] == jnp.arange(taps.shape[0]), taps, 0.0), -1)


def left(m):
    high, low = halves(m)
    return jnp.block([[high, high], [low, jnp.zeros_like(low)]])


def right(m):
    high, low = halves(m)
    return jnp.block([[high, low], [high, jnp.zeros_like(low)]])


def operators(kernels):
    k = kernels / jnp.sum(kernels, axis=1, keepdims=True)
    along_y = band(k[1], PLANE, PLANE, lambda a, b: a - b + 15)
    along_x = band(k[2], PLANE, PLANE, lambda a, b: a - b + 15)
    blur_z = band(k[0], 64, 96, lambda row, col: 31 - (col - row))
    return_z = band(k[0], BLOCK, 128, lambda row, col: col - row - 1)
    return (
        left(along_y), right(along_x.T), left(along_y.T), right(along_x),
        left(blur_z), left(return_z),
    )


def cost(flops, nbytes):
    return pl.CostEstimate(flops=int(flops), bytes_accessed=int(nbytes), transcendentals=0)


PARAMS = pltpu.CompilerParams(vmem_limit_bytes=VMEM)
SQUARE = pl.BlockSpec((256, 256), lambda *_: (0, 0))


def two_planes(first, second, along_y, along_x):
    h0, l0 = split(first)
    h1, l1 = split(second)
    planes = jnp.concatenate(
        [jnp.concatenate([h0, h1], 1), jnp.concatenate([l0, l1], 1)], 0
    )
    out = jnp.dot(along_y, planes, preferred_element_type=F32)
    high, low = split(out[:PLANE] + out[PLANE:])
    rows = jnp.concatenate(
        [
            jnp.concatenate([high[:, :PLANE], low[:, :PLANE]], 1),
            jnp.concatenate([high[:, PLANE:], low[:, PLANE:]], 1),
        ],
        0,
    )
    out = jnp.dot(rows, along_x, preferred_element_type=F32)
    out = out[:, :PLANE] + out[:, PLANE:]
    return out[:PLANE], out[PLANE:]


def lateral_body(in_ref, y_ref, x_ref, out_ref):
    along_y, along_x = y_ref[...], x_ref[...]
    for i in range(0, in_ref.shape[0], 2):
        out_ref[i], out_ref[i + 1] = two_planes(in_ref[i], in_ref[i + 1], along_y, along_x)


def lateral(volume, along_y, along_x, group=16):
    count = volume.shape[0]
    block = pl.BlockSpec((group, PLANE, PLANE), lambda i: (i, 0, 0))
    return pl.pallas_call(
        lateral_body,
        grid=(count // group,),
        in_specs=[block, SQUARE, SQUARE],
        out_specs=block,
        out_shape=jax.ShapeDtypeStruct(volume.shape, F32),
        name="blur_lateral",
        cost_estimate=cost(count / 2 * 2**27, count * 2**17),
        compiler_params=PARAMS,
    )(volume, along_y, along_x)


def place_edge(chunk):
    return 16 * chunk + jnp.where(chunk >= 2, 32, 0)


def pieces_body(place, rows, total, sc_ref, *refs):
    count = len(place)
    pieces, (y_ref, x_ref, out_hbm), (held, out, sem, out_sem) = (
        refs[: 2 * count], refs[2 * count : 2 * count + 3], refs[2 * count + 3 :],
    )
    view = sc_ref[0]
    copies = []
    for i in range(count):
        for half in range(2):
            copies.append(
                pltpu.make_async_copy(
                    pieces[2 * i + half],
                    held.at[pl.ds(i * rows, rows), pl.ds(64 * half, 64)],
                    sem.at[2 * i + half],
                )
            )
            copies[-1].start()
    along_y, along_x = y_ref[...], x_ref[...]
    outs = []
    for i in range(count):
        copies[2 * i].wait()
        copies[2 * i + 1].wait()

        @pl.loop(0, rows // 4)
        def _(j):
            for k in (0, 2):
                row = i * rows + 4 * j + k
                out[row], out[row + 1] = two_planes(held[row], held[row + 1], along_y, along_x)

        outs.append(
            pltpu.make_async_copy(
                out.at[pl.ds(i * rows, rows)],
                out_hbm.at[pl.ds(place[i](view), rows)],
                out_sem.at[i],
            )
        )
        outs[-1].start()
    for copy in outs:
        copy.wait()


def lateral_pieces(scalars, pieces, place, rows, along_y, along_x):
    count = len(pieces)
    total = count * rows
    anywhere = pl.BlockSpec(memory_space=pl.ANY)
    whole = pl.BlockSpec(memory_space=pltpu.VMEM)
    return pl.pallas_call(
        functools.partial(pieces_body, place, rows, total),
        in_specs=[pl.BlockSpec(memory_space=pltpu.SMEM)] + [anywhere] * (2 * count) + [whole] * 2,
        out_specs=anywhere,
        out_shape=jax.ShapeDtypeStruct((total, PLANE, PLANE), F32),
        scratch_shapes=[
            pltpu.VMEM((total, PLANE, PLANE), F32),
            pltpu.VMEM((total, PLANE, PLANE), F32),
            pltpu.SemaphoreType.DMA((2 * count,)),
            pltpu.SemaphoreType.DMA((count,)),
        ],
        name="blur_pieces",
        cost_estimate=cost(total / 2 * 2**27, total * 2**17),
        compiler_params=PARAMS,
    )(scalars, *[half for piece in pieces for half in piece], along_y, along_x)


def axial_body(segments, depth, sc_ref, *refs):
    count = len(segments)
    d_ref, blur_ref, back_ref, out_ref = refs[count:]
    blur_z, return_z = blur_ref[...], back_ref[...]
    start = sc_ref[2]
    for y in range(0, depth, 2):
        high, low = {}, {}
        for ref, places in zip(refs[:count], segments):
            for segment, row in places.items():
                rows = slice(row, row + 32)
                high[segment], low[segment] = split(
                    jnp.concatenate([ref[rows, y, :], ref[rows, y + 1, :]], 1)
                )
        blurred = []
        for first in (0, 2):
            window = jnp.concatenate(
                [high[first + i] for i in range(3)] + [low[first + i] for i in range(3)], 0
            )
            out = jnp.dot(blur_z, window, preferred_element_type=F32)
            blurred.append(out[:64] + out[64:])
        blurred = jnp.concatenate(blurred, 0) + BACKGROUND
        data = jnp.concatenate(
            [d_ref[pl.ds(start, 128), y, :], d_ref[pl.ds(start, 128), y + 1, :]], 1
        )
        quotient = jnp.concatenate(split(data / blurred), 0)
        out = jnp.dot(return_z, quotient, preferred_element_type=F32)
        out = out[:BLOCK] + out[BLOCK:]
        out_ref[:, y, :] = out[:, :PLANE]
        out_ref[:, y + 1, :] = out[:, PLANE:]


def axial(scalars, parts, segments, data, blur_z, return_z, depth=8):
    spec = lambda rows: pl.BlockSpec((rows, depth, PLANE), lambda i, sc: (0, i, 0))
    fixed = lambda m: pl.BlockSpec(m.shape, lambda i, sc: (0, 0))
    return pl.pallas_call(
        functools.partial(axial_body, segments, depth),
        grid_spec=pltpu.PrefetchScalarGridSpec(
            num_scalar_prefetch=1,
            grid=(PLANE // depth,),
            in_specs=[spec(part.shape[0]) for part in parts]
            + [spec(data.shape[0]), fixed(blur_z), fixed(return_z)],
            out_specs=spec(BLOCK),
        ),
        out_shape=jax.ShapeDtypeStruct((BLOCK, PLANE, PLANE), F32),
        name="quotient_axial",
        cost_estimate=cost(64 * 2**27, 400 * 2**16),
        compiler_params=PARAMS,
    )(scalars, *parts, data, blur_z, return_z)


def weighted_body(rows, place, sc_ref, r_ref, w_ref, y_ref, x_ref, *outs):
    step = pl.program_id(0)
    along_y, along_x = y_ref[...], x_ref[...]
    chunk = lax.rem(sc_ref[0] + chunk_step(step), 4)
    first = place(chunk)
    for which in range(4):

        @pl.when(step == which)
        def _():
            for i in range(0, rows, 2):
                pair = two_planes(r_ref[i], r_ref[i + 1], along_y, along_x)
                for k in range(2):
                    value = pair[k] * w_ref[i + k]
                    value = jnp.where(first + i + k >= sc_ref[1], value, 0.0)
                    outs[2 * which][i + k] = value[:64]
                    outs[2 * which + 1][i + k] = value[64:]


def chunk_step(step):
    return jnp.where(step == 0, 2, jnp.where(step == 1, 1, jnp.where(step == 2, 3, 0)))


def weighted(scalars, returned, weights, along_y, along_x, rows, place):
    block = pl.BlockSpec(
        (rows, PLANE, PLANE),
        lambda i, sc: (place(lax.rem(sc[0] + chunk_step(i), 4)) // rows, 0, 0),
    )
    piece = pl.BlockSpec((rows, 64, PLANE), lambda i, sc: (0, 0, 0))
    return pl.pallas_call(
        functools.partial(weighted_body, rows, place),
        grid_spec=pltpu.PrefetchScalarGridSpec(
            num_scalar_prefetch=1,
            grid=(4,),
            in_specs=[block, block, SQUARE, SQUARE],
            out_specs=[piece] * 8,
        ),
        out_shape=[jax.ShapeDtypeStruct((rows, 64, PLANE), F32)] * 8,
        name="return_lateral",
        cost_estimate=cost(2 * rows * 2**27, 12 * rows * 2**16),
        compiler_params=PARAMS,
    )(scalars, returned, weights, along_y, along_x)


def place_inner(chunk):
    return 32 + INNER * chunk


def pick_body(steps, sc_ref, w_ref, *refs):
    outs, sem = refs[:-1], refs[-1]
    copies = []
    for i, step in enumerate(steps):
        chunk = lax.rem(sc_ref[0] + step, 4)
        for half in range(2):
            side = pl.ds(64 * half, 64)
            for k, (row, rows, at) in enumerate(
                ((place_edge(chunk), EDGE, 0), (place_inner(chunk), INNER, EDGE))
            ):
                copies.append(
                    pltpu.make_async_copy(
                        w_ref.at[pl.ds(row, rows), side],
                        outs[2 * i + half].at[pl.ds(at, rows)],
                        sem.at[4 * i + 2 * half + k],
                    )
                )
                copies[-1].start()
    for copy in copies:
        copy.wait()


def pick(scalars, volume, steps):
    anywhere = pl.BlockSpec(memory_space=pl.ANY)
    return pl.pallas_call(
        functools.partial(pick_body, steps),
        in_specs=[pl.BlockSpec(memory_space=pltpu.SMEM), anywhere],
        out_specs=[anywhere] * (2 * len(steps)),
        out_shape=[jax.ShapeDtypeStruct((EDGE + INNER, 64, PLANE), F32)] * (2 * len(steps)),
        scratch_shapes=[pltpu.SemaphoreType.DMA((4 * len(steps),))],
        name="pick_chunks",
        cost_estimate=cost(0, len(steps) * 24 * 2**17),
        compiler_params=PARAMS,
    )(scalars, volume)


def assemble_body(sc_ref, *refs):
    pieces, out, sem = refs[:-2], refs[-2], refs[-1]
    copies = []
    for i in range(8):
        chunk = lax.rem(sc_ref[0] + STEP[i % 4], 4)
        row, rows = (place_edge(chunk), EDGE) if i < 4 else (place_inner(chunk), INNER)
        for half in range(2):
            copies.append(
                pltpu.make_async_copy(
                    pieces[2 * i + half],
                    out.at[pl.ds(row, rows), pl.ds(64 * half, 64)],
                    sem.at[2 * i + half],
                )
            )
            copies[-1].start()
    for copy in copies:
        copy.wait()


def assemble(scalars, edge, inner):
    anywhere = pl.BlockSpec(memory_space=pl.ANY)
    pieces = [half for piece in edge + inner for half in piece]
    return pl.pallas_call(
        assemble_body,
        in_specs=[pl.BlockSpec(memory_space=pltpu.SMEM)] + [anywhere] * 16,
        out_specs=anywhere,
        out_shape=jax.ShapeDtypeStruct((BLOCK, PLANE, PLANE), F32),
        scratch_shapes=[pltpu.SemaphoreType.DMA((16,))],
        name="assemble",
        cost_estimate=cost(0, 96 * 2**17),
        compiler_params=PARAMS,
    )(scalars, *pieces)


def to_plus(value):
    return lax.ppermute(value, "view", [(i, (i + 1) % 4) for i in range(4)])


def to_minus(value):
    return lax.ppermute(value, "view", [(i, (i - 1) % 4) for i in range(4)])


def to_space(value, steps):
    count = lax.axis_size("space")
    pairs = [(i, i + steps) for i in range(count) if 0 <= i + steps < count]
    return lax.ppermute(value, "space", pairs)


def to_rim(value, step):
    count = lax.axis_size("space")
    pairs = []
    for view in range(4):
        move = 1 if (view + step) % 4 >= 2 else -1
        for i in range(count):
            if 0 <= i + move < count:
                pairs.append((view * count + i, view * count + i + move))
    return lax.ppermute(value, ("view", "space"), pairs)


def ring_sum(pieces):
    far_a = to_plus(pieces[0])
    far_b = to_minus(pieces[1])
    left_b = to_plus(pieces[3])
    right_a = to_minus(pieces[4])
    left_a = to_plus(pieces[2] + far_a)
    right_b = to_minus(pieces[5] + far_b)
    return pieces[6] + left_a + right_a, pieces[7] + left_b + right_b


def ring_gather(own):
    own_a, own_b = own
    left_a, right_b = to_plus(own_a), to_minus(own_b)
    left_b, right_a = to_plus(own_b), to_minus(own_a)
    far_a, far_b = to_plus(left_a), to_minus(right_b)
    return [(far_a, far_b), (right_a, right_b), (left_a, left_b), (own_a, own_b)]


def on_device(estimate, view_data, blend_weights, kernels, shifts):
    view, place = lax.axis_index("view"), lax.axis_index("space")
    shift = shifts[0]
    scalars = jnp.stack([view, jnp.where(place == 0, shift, 0), 16 - shift]).astype(jnp.int32)
    data, weights = view_data[0], blend_weights[0]
    blur_y, blur_x, back_y, back_x, blur_z, back_z = operators(kernels[0])

    low = to_space(estimate[BLOCK - RIM :], 1)
    high = to_space(estimate[:RIM], -1)
    data_low = to_space(data[BLOCK - RIM :], 1)
    data_high = to_space(data[:16], -1)

    weight_sum = ring_sum(pick(scalars, weights, STEP))
    own = pick(scalars, estimate, (0,))

    parts = [lateral(part, blur_y, blur_x) for part in (low, estimate, high)]
    segments = [{0: 0}, {1: 0, 2: 32, 3: 64}, {4: 0}]
    data = jnp.concatenate([data_low, data, data_high], 0)

    for iteration in range(ITERS):
        returned = axial(scalars, parts, segments, data, blur_z, back_z)
        edge = weighted(scalars, returned, weights, back_y, back_x, EDGE, place_edge)
        inner = weighted(scalars, returned, weights, back_y, back_x, INNER, place_inner)
        edge, inner = ring_sum(edge), ring_sum(inner)
        own_edge = [e[:EDGE] * c / w[:EDGE] for e, c, w in zip(own, edge, weight_sum)]
        own_inner = [e[EDGE:] * c / w[EDGE:] for e, c, w in zip(own, inner, weight_sum)]
        own = [jnp.concatenate([e, i], 0) for e, i in zip(own_edge, own_inner)]
        edge, inner = ring_gather(own_edge), ring_gather(own_inner)
        if iteration == ITERS - 1:
            return assemble(scalars, edge, inner)
        rim = [tuple(to_rim(half, step) for half in piece) for piece, step in zip(edge, STEP)]

        def inside(step):
            return lambda v: 32 + EDGE * lax.rem(v + step, 4)

        def beyond(step):
            def at(v):
                chunk = lax.rem(v + step, 4)
                return jnp.where(chunk >= 2, EDGE * (chunk - 2), 96 + EDGE * chunk)
            return at

        def middle(step):
            return lambda v: INNER * lax.rem(v + step, 4)

        parts = [
            lateral_pieces(
                scalars, edge + rim, [inside(s) for s in STEP] + [beyond(s) for s in STEP],
                EDGE, blur_y, blur_x,
            ),
            lateral_pieces(scalars, inner, [middle(s) for s in STEP], INNER, blur_y, blur_x),
        ]
        segments = [{0: 0, 1: 32, 3: 64, 4: 96}, {2: 0}]


def solution(mesh):
    return jax.shard_map(
        on_device,
        mesh=mesh,
        in_specs=(
            P("space", None, None),
            P("view", "space", None, None),
            P("view", "space", None, None),
            P("view", None, None),
            P("view"),
        ),
        out_specs=P("space", None, None),
        check_vma=False,
    )
```

time: 694 us -> 657 us (0.947)
  Pallas kernels: 0 us -> 336 us
  waiting for transfers between devices: 446 us -> 173 us
  matrix products: 153 us -> 0 us
  starting transfers between devices: 22.4 us -> 103 us
  other arithmetic: 40.1 us -> 18 us
  between operations: 14.7 us -> 2.02 us
    psum x2 -> x0, waiting for transfers between devices: 365 us -> none  [the longest x1 234 us: on_device(): weight_sum = lax.psum(weights, 'view')]
    pallas_call x0 -> x14, Pallas kernels: none -> 336 us  [the longest x2 147 us: pick(): pl.pallas_call(functools.partial(pick_body, steps), in_specs=[pl.BlockSpe...]
    dot_general x12 -> x0, matrix products: 153 us -> none  [the longest x4 54.5 us: transverse(): jnp.einsum('ab,zbx->zax', across_y, volume, precision=lax.Precision.HIGHEST)]
    ppermute x8 -> x66, waiting for transfers between devices: 81.1 us -> 173 us  [the longest x27 86.7 us: to_minus(): return lax.ppermute(value, 'view', [(i, (i - 1) % 4) for i in range(4)])]
    ppermute x8 -> x66, starting transfers between devices: 22.4 us -> 103 us  [the longest x27 52.6 us: to_minus(): return lax.ppermute(value, 'view', [(i, (i - 1) % 4) for i in range(4)])]
    div x3 -> x9, other arithmetic: 20.5 us -> 1.34 us  [the longest x4 0.89 us: on_device(): e[:EDGE] * c / w[:EDGE]]
    mul x2 -> x0, other arithmetic: 7.86 us -> none  [on_device(): weighted = weights * correction]
  transfers between devices with their start and end apart: 10 -> 66, of which waited for: 8 -> 22; matrix products, arithmetic and copies ran while one was open for 6% -> 4% of each run, Pallas kernels for 0% -> 32%
where the time goes in v1:
time: 657 us; the launch traced here: 646 us
  Pallas kernels  336 us (51%)
  waiting for transfers between devices  173 us (26%)
  starting transfers between devices  103 us (16%)
  other arithmetic  18 us (3%)
  local copies, waits for them, and re-layouts  14.6 us (2%)
    pallas_call x2, Pallas kernels, pick(): pl.pallas_call(functools.partial(pick_body, steps), in_specs=[pl.BlockSpe...  147 us
    ppermute x27, waiting for transfers between devices, to_minus(): return lax.ppermute(value, 'view', [(i, (i - 1) % 4) for i in range(4)])  86.7 us
    pallas_call x1, Pallas kernels, assemble(): pl.pallas_call(assemble_body, in_specs=[pl.BlockSpec(memory_space=pltpu.S...  81.2 us
    ppermute x27, waiting for transfers between devices, to_plus(): return lax.ppermute(value, 'view', [(i, (i + 1) % 4) for i in range(4)])  80.8 us
    ppermute x27, starting transfers between devices, to_minus(): return lax.ppermute(value, 'view', [(i, (i - 1) % 4) for i in range(4)])  52.6 us
    pallas_call x2, Pallas kernels, axial(): pl.pallas_call(functools.partial(axial_body, segments, depth), grid_spec=...  46.8 us
    pallas_call x4, Pallas kernels, weighted(): pl.pallas_call(functools.partial(weighted_body, rows, place), grid_spec=p...  24.6 us
    ppermute x8, starting transfers between devices, to_rim(): return lax.ppermute(value, ('view', 'space'), pairs)  23.1 us
  transfers between devices with their start and end apart: 66, of which 22 were waited for; matrix products, arithmetic and copies ran while one was open for 4% of the time, Pallas kernels for 32%

profile of v1, /device:TPU:96, one launch (start us, length us, event | category | flops | bytes accessed | tf_op | source)
XLA Modules:
  0.0 646.4 jit_solution(10109453674125182254)
XLA Ops:
  0.0 3.1 slice_bitcast_fusion
  5.0 4.9 fusion.18
  10.0 3.6 collective-permute-start.1
  16.3 144.7 %pick_chunks.3 = (f32[24,64,128]{2,1,0:T(8,128)S(1)}, f32[24,64,128]{2,1,0:T(8,128)}, f32[24,64,128]{2,1,0:T(8,128)S(1)}, f32[24,64,128]{2,1,0:T(8,128)}, f32[24...) custom-call(s32[3]{0:T(128)S(1)} %pad_add_fusion.sc_ref, ...), custom_call_target="tpu_custom_call" | custom-call | bytes 12582912 | tf_op jit(solution)/shard_map/pick_chunks/pallas_call | solution.py:296
  167.2 14.0 %collective-permute-done.7 = f32[24,64,128]{2,1,0:T(8,128)S(1)} collective-permute-done((f32[24,64,128]{2,1,0:T(8,128)S(1)}, f32[24,64,128]{2,1,0:T(8,128)S(1)}, u32[]{:S(2)}, u32[]{:S(2)}) %collective-permute-start.7) | collective-permute-done | bytes 786464 | tf_op jit(solution)/shard_map/ppermute | solution.py:343
  181.2 3.2 collective-permute-start.3
  186.5 9.1 %blur_lateral.4.refs_1_ = f32[96,128,128]{2,1,0:T(8,128)} custom-call(f32[96,128,128]{2,1,0:T(8,128)} %in_ref.1, bf16[256,256]{1,0:T(8,128)(2,1)S(1)} %fusion.5.y_ref.refs_16_.refs_8_, bf16[256,256]{1,0:T(8,128)(2,1)S(1)} %fusion.6.x_ref.refs_17_.refs_9_), custom_call_target="tpu_custom_call" | custom-call | flops 6442450944 | bytes 12582912 | tf_op jit(solution)/shard_map/blur_lateral/pallas_call | solution.py:96
  196.6 2.2 collective-permute-start.9
  198.8 2.2 add.128
  201.0 3.0 blur_lateral.5.refs_2_
  205.9 3.0 blur_lateral.3.refs_0_
  210.2 2.7 collective-permute-start.17
  212.9 8.8 %pad_maximum_fusion.refs_3_.refs_2_ = f32[144,128,128]{2,1,0:T(8,128)} fusion(f32[16,128,128]{2,1,0:T(8,128)} %collective-permute-done.3, f32[96,128,128]{2,1,0:T(8,128)} %bitcast.31, f32[32,128,128]{2,1,0:T(8,128)} %collective-permute-done.2), kind=kLoop, calls=%fused_computation | loop fusion | flops 4718592 | bytes 18874368 | tf_op jit(solution)/shard_map/concatenate | solution.py:402
  223.3 23.5 %quotient_axial.2.r_ref = f32[96,128,128]{2,1,0:T(8,128)} custom-call(s32[3]{0:T(128)S(1)} %pad_add_fusion.sc_ref, f32[32,128,128]{2,1,0:T(8,128)S(1)} %copy-done.3, f32[96,128,128]{2,1,0:T(8,128)} %blur_lateral.4.refs_1_, f32[32,128,128]{2,1,0:T(8,128)} %copy-done.1, f32[144,128,128]{2,1,0:T(8,128)} %pad_maximum_fusion.refs_3_.refs_2_, ...), custom_call_target="tpu_custom_call" | custom-call | flops 8589934592 | bytes 26214400 | tf_op jit(solution)/shard_map/quotient_axial/pallas_call | solution.py:209
  246.7 5.0 return_lateral.5
  252.0 7.3 %return_lateral.4 = (f32[16,64,128]{2,1,0:T(8,128)S(1)}, f32[16,64,128]{2,1,0:T(8,128)S(1)}, f32[16,64,128]{2,1,0:T(8,128)S(1)}, f32[16,64,128]{2,1,0:T(8,128)S(...) custom-call(s32[3]{0:T(128)S(1)} %pad_add_fusion.sc_ref, ...), custom_call_target="tpu_custom_call" | custom-call | flops 4294967296 | bytes 12582912 | tf_op jit(solution)/shard_map/return_lateral/pallas_call | solution.py:253
  262.4 2.0 collective-permute-start.32
  264.4 1.9 collective-permute-start.36
  269.8 7.5 %collective-permute-done.36 = f32[8,64,128]{2,1,0:T(8,128)S(1)} collective-permute-done((f32[8,64,128]{2,1,0:T(8,128)S(1)}, f32[8,64,128]{2,1,0:T(8,128)S(1)}, u32[]{:S(2)}, u32[]{:S(2)}) %collective-permute-start.36) | collective-permute-done | bytes 262176 | tf_op jit(solution)/shard_map/ppermute | solution.py:347
  277.3 2.0 collective-permute-start.35
  280.8 2.0 collective-permute-start.37
  282.9 5.6 collective-permute-done.13
  288.6 2.0 collective-permute-start.12
  291.9 13.5 %collective-permute-done.37 = f32[8,64,128]{2,1,0:T(8,128)S(1)} collective-permute-done((f32[8,64,128]{2,1,0:T(8,128)S(1)}, f32[8,64,128]{2,1,0:T(8,128)S(1)}, u32[]{:S(2)}, u32[]{:S(2)}) %collective-permute-start.37) | collective-permute-done | bytes 262176 | tf_op jit(solution)/shard_map/ppermute | solution.py:347
  305.4 3.1 collective-permute-start.14
  309.9 2.5 collective-permute-start.38
  312.3 6.1 collective-permute-done.33.refs_4_
  318.5 3.8 collective-permute-done.14
  324.4 3.2 collective-permute-start.20
  327.6 3.2 collective-permute-start.18
  331.2 24.8 %collective-permute-done.39.refs_1_ = f32[8,64,128]{2,1,0:T(8,128)S(1)} collective-permute-done((f32[8,64,128]{2,1,0:T(8,128)S(1)}, f32[8,64,128]{2,1,0:T(8,128)S(1)}, u32[]{:S(2)}, u32[]{:S(2)}) %collective-permute-start.39) | collective-permute-done | bytes 262176 | tf_op jit(solution)/shard_map/ppermute | solution.py:347
  356.0 2.8 collective-permute-start.29
  360.1 2.0 collective-permute-start.24
  362.1 2.2 collective-permute-start.11
  365.5 5.9 collective-permute-start.26
  371.4 3.0 collective-permute-done.21.refs_5_
  374.4 2.5 collective-permute-start.25
  377.0 2.8 collective-permute-start.27
  379.7 5.9 collective-permute-done.11.refs_0_
  385.6 2.4 collective-permute-start.22
  388.1 2.7 collective-permute-start.23
  390.7 5.2 blur_pieces.3.refs_1_
  396.2 5.6 collective-permute-done.23.refs_9_
  401.9 16.4 %blur_pieces.2.refs_0_ = f32[128,128,128]{2,1,0:T(8,128)} custom-call(s32[3]{0:T(128)S(1)} %pad_add_fusion.sc_ref, f32[16,64,128]{2,1,0:T(8,128)S(1)} %collective-permute-done.11.refs_0_, f32[16,64,128]{2,1,0:T(8,128)S(1)} %collective-permute-done.19.refs_1_, f32[16,64,128]{2,1,0:T(8,128)S(1)} %collective-permute-done.20.refs_2_, ...), custom_call_target="tpu_custom_call" | custom-call | flops 8589934592 | bytes 16777216 | tf_op jit(solution)/shard_map/blur_pieces/pallas_call | solution.py:158
  418.2 23.3 %quotient_axial.3.r_ref = f32[96,128,128]{2,1,0:T(8,128)} custom-call(s32[3]{0:T(128)S(1)} %pad_add_fusion.sc_ref, f32[128,128,128]{2,1,0:T(8,128)} %blur_pieces.2.refs_0_, f32[32,128,128]{2,1,0:T(8,128)S(1)} %copy-done, f32[144,128,128]{2,1,0:T(8,128)} %pad_maximum_fusion.refs_3_.refs_2_, bf16[128,192]{1,0:T(8,128)(2,1)S(1)} %fusion.15.refs_4_.refs_3_, ...), custom_call_target="tpu_custom_call" | custom-call | flops 8589934592 | bytes 26214400 | tf_op jit(solution)/shard_map/quotient_axial/pallas_call | solution.py:209
  441.5 7.3 %return_lateral.6 = (f32[16,64,128]{2,1,0:T(8,128)S(1)}, f32[16,64,128]{2,1,0:T(8,128)S(1)}, f32[16,64,128]{2,1,0:T(8,128)S(1)}, f32[16,64,128]{2,1,0:T(8,128)S(...) custom-call(s32[3]{0:T(128)S(1)} %pad_add_fusion.sc_ref, ...), custom_call_target="tpu_custom_call" | custom-call | flops 4294967296 | bytes 12582912 | tf_op jit(solution)/shard_map/return_lateral/pallas_call | solution.py:253
  448.9 3.5 collective-permute-start.48
  452.3 5.0 return_lateral.7
  457.4 3.2 collective-permute-start.60
  460.6 8.9 %collective-permute-done.54 = f32[8,64,128]{2,1,0:T(8,128)S(1)} collective-permute-done((f32[8,64,128]{2,1,0:T(8,128)S(1)}, f32[8,64,128]{2,1,0:T(8,128)S(1)}, u32[]{:S(2)}, u32[]{:S(2)}) %collective-permute-start.54) | collective-permute-done | bytes 262176 | tf_op jit(solution)/shard_map/ppermute | solution.py:343
  469.6 3.2 collective-permute-start.44
  473.2 2.0 collective-permute-done.56
  475.2 4.8 collective-permute-done.55
  480.1 6.3 collective-permute-done.44
  486.5 3.7 collective-permute-start.61
  491.5 16.4 %collective-permute-done.47 = f32[16,64,128]{2,1,0:T(8,128)S(1)} collective-permute-done((f32[16,64,128]{2,1,0:T(8,128)S(1)}, f32[16,64,128]{2,1,0:T(8,128)S(1)}, u32[]{:S(2)}, u32[]{:S(2)}) %collective-permute-start.47) | collective-permute-done | bytes 524320 | tf_op jit(solution)/shard_map/ppermute | solution.py:343
  508.2 3.3 collective-permute-start.50
  511.7 3.2 collective-permute-start.62
  514.9 3.4 collective-permute-done.57.refs_12_
  518.3 16.8 %collective-permute-done.65.refs_13_ = f32[8,64,128]{2,1,0:T(8,128)S(1)} collective-permute-done((f32[8,64,128]{2,1,0:T(8,128)S(1)}, f32[8,64,128]{2,1,0:T(8,128)S(1)}, u32[]{:S(2)}, u32[]{:S(2)}) %collective-permute-start.65) | collective-permute-done | bytes 262176 | tf_op jit(solution)/shard_map/ppermute | solution.py:343
  535.2 2.0 collective-permute-start.53
  537.3 3.2 collective-permute-start.51
  540.8 23.1 %collective-permute-done.63.refs_9_ = f32[8,64,128]{2,1,0:T(8,128)S(1)} collective-permute-done((f32[8,64,128]{2,1,0:T(8,128)S(1)}, f32[8,64,128]{2,1,0:T(8,128)S(1)}, u32[]{:S(2)}, u32[]{:S(2)}) %collective-permute-start.63) | collective-permute-done | bytes 262176 | tf_op jit(solution)/shard_map/ppermute | solution.py:347
  564.7 81.2 %assemble.1 = f32[96,128,128]{2,1,0:T(8,128)} custom-call(s32[3]{0:T(128)S(1)} %pad_add_fusion.sc_ref, f32[16,64,128]{2,1,0:T(8,128)S(1)} %collective-permute-done.46.refs_0_, f32[16,64,128]{2,1,0:T(8,128)S(1)} %collective-permute-done.51.refs_1_, f32[16,64,128]{2,1,0:T(8,128)S(1)} %collective-permute-done.52.refs_2_, f32[16,64,128]{2,1,0:T(8,128)} %copy-done.14, ...), custom_call_target="tpu_custom_call" | custom-call | bytes 12582912 | tf_op jit(solution)/shard_map/assemble/pallas_call | solution.py:330
  (179 shorter events, 37.4 us)
Async XLA Ops:
  3.1 209.8 %collective-permute-start.2 = (f32[32,128,128]{2,1,0:T(8,128)}, f32[32,128,128]{2,1,0:T(8,128)}, u32[]{:S(2)}, u32[]{:S(2)}) collective-permute-start(f32[32,128,128]{2,1,0:T(8,128)} %slice_bitcast_fusion), channel_id=1, source_target_pairs={{0,1},{1,2},{2,3},{3,4},{4,5},{5,6},{6,7},{7,8},{8,9},{9,10},{10,1... | collective-permute-start | bytes 6291464 | tf_op jit(solution)/shard_map/ppermute | solution.py:353
  10.0 191.1 %collective-permute-start.1 = (f32[32,128,128]{2,1,0:T(8,128)}, f32[32,128,128]{2,1,0:T(8,128)}, u32[]{:S(2)}, u32[]{:S(2)}) collective-permute-start(f32[32,128,128]{2,1,0:T(8,128)} %get-tuple-element.91), channel_id=1, source_target_pairs={{1,0},{2,1},{3,2},{4,3},{5,4},{6,5},{7,6},{8,7},{9,8},{10,9},{11,1... | collective-permute-start | bytes 6291464 | tf_op jit(solution)/shard_map/ppermute | solution.py:353
  13.6 191.7 %collective-permute-start = (f32[32,128,128]{2,1,0:T(8,128)}, f32[32,128,128]{2,1,0:T(8,128)}, u32[]{:S(2)}, u32[]{:S(2)}) collective-permute-start(f32[32,128,128]{2,1,0:T(8,128)} %get-tuple-element.92), channel_id=1, source_target_pairs={{0,1},{1,2},{2,3},{3,4},{4,5},{5,6},{6,7},{7,8},{8,9},{9,10},{10,1... | collective-permute-start | bytes 6291464 | tf_op jit(solution)/shard_map/ppermute | solution.py:353
  161.0 20.2 %collective-permute-start.7 = (f32[24,64,128]{2,1,0:T(8,128)S(1)}, f32[24,64,128]{2,1,0:T(8,128)S(1)}, u32[]{:S(2)}, u32[]{:S(2)}) collective-permute-start(f32[24,64,128]{2,1,0:T(8,128)S(1)} %get-tuple-element.54), channel_id=1, source_target_pairs={{0,32},{32,64},{64,96},{96,0},{1,33},{33,65},{65,97},{97,1},{2,34}... | collective-permute-start | bytes 2359304 | tf_op jit(solution)/shard_map/ppermute | solution.py:343
  162.7 34.0 %collective-permute-start.16 = (f32[24,64,128]{2,1,0:T(8,128)}, f32[24,64,128]{2,1,0:T(8,128)}, u32[]{:S(2)}, u32[]{:S(2)}) collective-permute-start(f32[24,64,128]{2,1,0:T(8,128)} %get-tuple-element.64), channel_id=1, source_target_pairs={{0,96},{32,0},{64,32},{96,64},{1,97},{33,1},{65,33},{97,65},{2,98}... | collective-permute-start | bytes 2359304 | tf_op jit(solution)/shard_map/ppermute | solution.py:347
  181.2 29.0 %collective-permute-start.3 = (f32[16,128,128]{2,1,0:T(8,128)S(1)}, f32[16,128,128]{2,1,0:T(8,128)}, u32[]{:S(2)}, u32[]{:S(2)}) collective-permute-start(f32[16,128,128]{2,1,0:T(8,128)S(1)} %slice_bitcast_fusion.1), channel_id=1, source_target_pairs={{1,0},{2,1},{3,2},{4,3},{5,4},{6,5},{7,6},{8,7},{9,8},{10,9},{11,1... | collective-permute-start | bytes 3145736 | tf_op jit(solution)/shard_map/ppermute | solution.py:353
  196.6 62.7 %collective-permute-start.9 = (f32[24,64,128]{2,1,0:T(8,128)}, f32[24,64,128]{2,1,0:T(8,128)}, u32[]{:S(2)}, u32[]{:S(2)}) collective-permute-start(f32[24,64,128]{2,1,0:T(8,128)} %get-tuple-element.55), channel_id=1, source_target_pairs={{0,96},{32,0},{64,32},{96,64},{1,97},{33,1},{65,33},{97,65},{2,98}... | collective-permute-start | bytes 2359304 | tf_op jit(solution)/shard_map/ppermute | solution.py:347
  201.0 65.3 %collective-permute-start.15 = (f32[24,64,128]{2,1,0:T(8,128)}, f32[24,64,128]{2,1,0:T(8,128)S(1)}, u32[]{:S(2)}, u32[]{:S(2)}) collective-permute-start(f32[24,64,128]{2,1,0:T(8,128)} %get-tuple-element.62), channel_id=1, source_target_pairs={{0,32},{32,64},{64,96},{96,0},{1,33},{33,65},{65,97},{97,1},{2,34}... | collective-permute-start | bytes 2359304 | tf_op jit(solution)/shard_map/ppermute | solution.py:343
  205.4 55.4 %collective-permute-start.8 = (f32[24,64,128]{2,1,0:T(8,128)}, f32[24,64,128]{2,1,0:T(8,128)}, u32[]{:S(2)}, u32[]{:S(2)}) collective-permute-start(f32[24,64,128]{2,1,0:T(8,128)} %add.121), channel_id=1, source_target_pairs={{0,32},{32,64},{64,96},{96,0},{1,33},{33,65},{65,97},{97,1},{2,34}... | collective-permute-start | bytes 2359304 | tf_op jit(solution)/shard_map/ppermute | solution.py:343
  210.2 57.0 %collective-permute-start.17 = (f32[24,64,128]{2,1,0:T(8,128)}, f32[24,64,128]{2,1,0:T(8,128)}, u32[]{:S(2)}, u32[]{:S(2)}) collective-permute-start(f32[24,64,128]{2,1,0:T(8,128)} %add.128), channel_id=1, source_target_pairs={{0,96},{32,0},{64,32},{96,64},{1,97},{33,1},{65,33},{97,65},{2,98}... | collective-permute-start | bytes 2359304 | tf_op jit(solution)/shard_map/ppermute | solution.py:347
  251.7 12.6 %collective-permute-start.30 = (f32[8,64,128]{2,1,0:T(8,128)S(1)}, f32[8,64,128]{2,1,0:T(8,128)S(1)}, u32[]{:S(2)}, u32[]{:S(2)}) collective-permute-start(f32[8,64,128]{2,1,0:T(8,128)S(1)} %get-tuple-element.67), channel_id=1, source_target_pairs={{0,32},{32,64},{64,96},{96,0},{1,33},{33,65},{65,97},{97,1},{2,34}... | collective-permute-start | bytes 786440 | tf_op jit(solution)/shard_map/ppermute | solution.py:343
  259.3 20.0 %collective-permute-start.4 = (f32[16,64,128]{2,1,0:T(8,128)S(1)}, f32[16,64,128]{2,1,0:T(8,128)S(1)}, u32[]{:S(2)}, u32[]{:S(2)}) collective-permute-start(f32[16,64,128]{2,1,0:T(8,128)S(1)} %get-tuple-element.50), channel_id=1, source_target_pairs={{0,32},{32,64},{64,96},{96,0},{1,33},{33,65},{65,97},{97,1},{2,34}... | collective-permute-start | bytes 1572872 | tf_op jit(solution)/shard_map/ppermute | solution.py:343
  262.4 18.4 %collective-permute-start.32 = (f32[8,64,128]{2,1,0:T(8,128)S(1)}, f32[8,64,128]{2,1,0:T(8,128)S(1)}, u32[]{:S(2)}, u32[]{:S(2)}) collective-permute-start(f32[8,64,128]{2,1,0:T(8,128)S(1)} %get-tuple-element.68), channel_id=1, source_target_pairs={{0,96},{32,0},{64,32},{96,64},{1,97},{33,1},{65,33},{97,65},{2,98}... | collective-permute-start | bytes 786440 | tf_op jit(solution)/shard_map/ppermute | solution.py:347
  264.4 12.9 %collective-permute-start.36 = (f32[8,64,128]{2,1,0:T(8,128)S(1)}, f32[8,64,128]{2,1,0:T(8,128)S(1)}, u32[]{:S(2)}, u32[]{:S(2)}) collective-permute-start(f32[8,64,128]{2,1,0:T(8,128)S(1)} %get-tuple-element.72), channel_id=1, source_target_pairs={{0,96},{32,0},{64,32},{96,64},{1,97},{33,1},{65,33},{97,65},{2,98}... | collective-permute-start | bytes 786440 | tf_op jit(solution)/shard_map/ppermute | solution.py:347
  266.3 22.2 %collective-permute-start.13 = (f32[16,64,128]{2,1,0:T(8,128)S(1)}, f32[16,64,128]{2,1,0:T(8,128)S(1)}, u32[]{:S(2)}, u32[]{:S(2)}) collective-permute-start(f32[16,64,128]{2,1,0:T(8,128)S(1)} %get-tuple-element.60), channel_id=1, source_target_pairs={{0,96},{32,0},{64,32},{96,64},{1,97},{33,1},{65,33},{97,65},{2,98}... | collective-permute-start | bytes 1572872 | tf_op jit(solution)/shard_map/ppermute | solution.py:347
  267.2 15.5 %collective-permute-start.31 = (f32[8,64,128]{2,1,0:T(8,128)S(1)}, f32[8,64,128]{2,1,0:T(8,128)S(1)}, u32[]{:S(2)}, u32[]{:S(2)}) collective-permute-start(f32[8,64,128]{2,1,0:T(8,128)S(1)} %add.130), channel_id=1, source_target_pairs={{0,32},{32,64},{64,96},{96,0},{1,33},{33,65},{65,97},{97,1},{2,34}... | collective-permute-start | bytes 786440 | tf_op jit(solution)/shard_map/ppermute | solution.py:343
  277.3 13.3 %collective-permute-start.35 = (f32[8,64,128]{2,1,0:T(8,128)S(1)}, f32[8,64,128]{2,1,0:T(8,128)S(1)}, u32[]{:S(2)}, u32[]{:S(2)}) collective-permute-start(f32[8,64,128]{2,1,0:T(8,128)S(1)} %get-tuple-element.70), channel_id=1, source_target_pairs={{0,32},{32,64},{64,96},{96,0},{1,33},{33,65},{65,97},{97,1},{2,34}... | collective-permute-start | bytes 786440 | tf_op jit(solution)/shard_map/ppermute | solution.py:343
  279.4 29.2 %collective-permute-start.6 = (f32[16,64,128]{2,1,0:T(8,128)S(1)}, f32[16,64,128]{2,1,0:T(8,128)S(1)}, u32[]{:S(2)}, u32[]{:S(2)}) collective-permute-start(f32[16,64,128]{2,1,0:T(8,128)S(1)} %get-tuple-element.51), channel_id=1, source_target_pairs={{0,96},{32,0},{64,32},{96,64},{1,97},{33,1},{65,33},{97,65},{2,98}... | collective-permute-start | bytes 1572872 | tf_op jit(solution)/shard_map/ppermute | solution.py:347
  280.8 24.6 %collective-permute-start.37 = (f32[8,64,128]{2,1,0:T(8,128)S(1)}, f32[8,64,128]{2,1,0:T(8,128)S(1)}, u32[]{:S(2)}, u32[]{:S(2)}) collective-permute-start(f32[8,64,128]{2,1,0:T(8,128)S(1)} %add.134), channel_id=1, source_target_pairs={{0,96},{32,0},{64,32},{96,64},{1,97},{33,1},{65,33},{97,65},{2,98}... | collective-permute-start | bytes 786440 | tf_op jit(solution)/shard_map/ppermute | solution.py:347
  282.7 26.0 %collective-permute-start.5 = (f32[16,64,128]{2,1,0:T(8,128)S(1)}, f32[16,64,128]{2,1,0:T(8,128)S(1)}, u32[]{:S(2)}, u32[]{:S(2)}) collective-permute-start(f32[16,64,128]{2,1,0:T(8,128)S(1)} %add.118), channel_id=1, source_target_pairs={{0,32},{32,64},{64,96},{96,0},{1,33},{33,65},{65,97},{97,1},{2,34}... | collective-permute-start | bytes 1572872 | tf_op jit(solution)/shard_map/ppermute | solution.py:343
  288.6 21.3 %collective-permute-start.12 = (f32[16,64,128]{2,1,0:T(8,128)S(1)}, f32[16,64,128]{2,1,0:T(8,128)S(1)}, u32[]{:S(2)}, u32[]{:S(2)}) collective-permute-start(f32[16,64,128]{2,1,0:T(8,128)S(1)} %get-tuple-element.58), channel_id=1, source_target_pairs={{0,32},{32,64},{64,96},{96,0},{1,33},{33,65},{65,97},{97,1},{2,34}... | collective-permute-start | bytes 1572872 | tf_op jit(solution)/shard_map/ppermute | solution.py:343
  290.6 33.8 %collective-permute-start.40 = (f32[8,64,128]{2,1,0:T(8,128)S(1)}, f32[8,64,128]{2,1,0:T(8,128)S(1)}, u32[]{:S(2)}, u32[]{:S(2)}) collective-permute-start(f32[8,64,128]{2,1,0:T(8,128)S(1)} %multiply_divide_fusion.7.refs_6_), channel_id=1, source_target_pairs={{0,96},{32,0},{64,32},{96,64},{1,97},{33,1},{65,33},{97,65},{2,98}... | collective-permute-start | bytes 786440 | tf_op jit(solution)/shard_map/ppermute | solution.py:347
  305.4 16.9 %collective-permute-start.14 = (f32[16,64,128]{2,1,0:T(8,128)S(1)}, f32[16,64,128]{2,1,0:T(8,128)S(1)}, u32[]{:S(2)}, u32[]{:S(2)}) collective-permute-start(f32[16,64,128]{2,1,0:T(8,128)S(1)} %add.125), channel_id=1, source_target_pairs={{0,96},{32,0},{64,32},{96,64},{1,97},{33,1},{65,33},{97,65},{2,98}... | collective-permute-start | bytes 1572872 | tf_op jit(solution)/shard_map/ppermute | solution.py:347
  308.7 18.9 %collective-permute-start.41 = (f32[8,64,128]{2,1,0:T(8,128)S(1)}, f32[8,64,128]{2,1,0:T(8,128)S(1)}, u32[]{:S(2)}, u32[]{:S(2)}) collective-permute-start(f32[8,64,128]{2,1,0:T(8,128)S(1)} %multiply_divide_fusion.6.refs_7_), channel_id=1, source_target_pairs={{0,32},{32,64},{64,96},{96,0},{1,33},{33,65},{65,97},{97,1},{2,34}... | collective-permute-start | bytes 786440 | tf_op jit(solution)/shard_map/ppermute | solution.py:343
  309.9 17.8 %collective-permute-start.38 = (f32[8,64,128]{2,1,0:T(8,128)S(1)}, f32[8,64,128]{2,1,0:T(8,128)S(1)}, u32[]{:S(2)}, u32[]{:S(2)}) collective-permute-start(f32[8,64,128]{2,1,0:T(8,128)S(1)} %multiply_divide_fusion.6.refs_7_), channel_id=1, source_target_pairs={{0,96},{32,0},{64,32},{96,64},{1,97},{33,1},{65,33},{97,65},{2,98}... | collective-permute-start | bytes 786440 | tf_op jit(solution)/shard_map/ppermute | solution.py:347
  318.5 12.4 %collective-permute-start.34 = (f32[8,64,128]{2,1,0:T(8,128)S(1)}, f32[8,64,128]{2,1,0:T(8,128)S(1)}, u32[]{:S(2)}, u32[]{:S(2)}) collective-permute-start(f32[8,64,128]{2,1,0:T(8,128)S(1)} %collective-permute-done.33.refs_4_), channel_id=1, source_target_pairs={{0,32},{32,64},{64,96},{96,0},{1,33},{33,65},{65,97},{97,1},{2,34}... | collective-permute-start | bytes 786440 | tf_op jit(solution)/shard_map/ppermute | solution.py:343
  322.3 36.6 %collective-permute-start.28 = (f32[16,64,128]{2,1,0:T(8,128)S(1)}, f32[16,64,128]{2,1,0:T(8,128)S(1)}, u32[]{:S(2)}, u32[]{:S(2)}) collective-permute-start(f32[16,64,128]{2,1,0:T(8,128)S(1)} %multiply_divide_fusion.3.refs_6_), channel_id=1, source_target_pairs={{1,0},{2,1},{3,2},{4,3},{5,4},{6,5},{7,6},{8,7},{9,8},{10,9},{11,1... | collective-permute-start | bytes 1572872 | tf_op jit(solution)/shard_map/ppermute | solution.py:364
  324.4 35.6 %collective-permute-start.20 = (f32[16,64,128]{2,1,0:T(8,128)S(1)}, f32[16,64,128]{2,1,0:T(8,128)S(1)}, u32[]{:S(2)}, u32[]{:S(2)}) collective-permute-start(f32[16,64,128]{2,1,0:T(8,128)S(1)} %multiply_divide_fusion.3.refs_6_), channel_id=1, source_target_pairs={{0,96},{32,0},{64,32},{96,64},{1,97},{33,1},{65,33},{97,65},{2,98}... | collective-permute-start | bytes 1572872 | tf_op jit(solution)/shard_map/ppermute | solution.py:347
  327.6 34.5 %collective-permute-start.10 = (f32[16,64,128]{2,1,0:T(8,128)S(1)}, f32[16,64,128]{2,1,0:T(8,128)S(1)}, u32[]{:S(2)}, u32[]{:S(2)}) collective-permute-start(f32[16,64,128]{2,1,0:T(8,128)S(1)} %multiply_divide_fusion.3.refs_6_), channel_id=1, source_target_pairs={{0,32},{32,64},{64,96},{96,0},{1,33},{33,65},{65,97},{97,1},{2,34}... | collective-permute-start | bytes 1572872 | tf_op jit(solution)/shard_map/ppermute | solution.py:343
  327.6 36.7 %collective-permute-start.18 = (f32[16,64,128]{2,1,0:T(8,128)S(1)}, f32[16,64,128]{2,1,0:T(8,128)S(1)}, u32[]{:S(2)}, u32[]{:S(2)}) collective-permute-start(f32[16,64,128]{2,1,0:T(8,128)S(1)} %multiply_divide_fusion.2.refs_7_), channel_id=1, source_target_pairs={{0,96},{32,0},{64,32},{96,64},{1,97},{33,1},{65,33},{97,65},{2,98}... | collective-permute-start | bytes 1572872 | tf_op jit(solution)/shard_map/ppermute | solution.py:347
  330.9 25.1 %collective-permute-start.39 = (f32[8,64,128]{2,1,0:T(8,128)S(1)}, f32[8,64,128]{2,1,0:T(8,128)S(1)}, u32[]{:S(2)}, u32[]{:S(2)}) collective-permute-start(f32[8,64,128]{2,1,0:T(8,128)S(1)} %collective-permute-done.38.refs_3_), channel_id=1, source_target_pairs={{0,96},{32,0},{64,32},{96,64},{1,97},{33,1},{65,33},{97,65},{2,98}... | collective-permute-start | bytes 786440 | tf_op jit(solution)/shard_map/ppermute | solution.py:347
  358.8 15.6 %collective-permute-start.21 = (f32[16,64,128]{2,1,0:T(8,128)S(1)}, f32[16,64,128]{2,1,0:T(8,128)S(1)}, u32[]{:S(2)}, u32[]{:S(2)}) collective-permute-start(f32[16,64,128]{2,1,0:T(8,128)S(1)} %multiply_divide_fusion.2.refs_7_), channel_id=1, source_target_pairs={{0,32},{32,64},{64,96},{96,0},{1,33},{33,65},{65,97},{97,1},{2,34}... | collective-permute-start | bytes 1572872 | tf_op jit(solution)/shard_map/ppermute | solution.py:343
  360.1 16.9 %collective-permute-start.24 = (f32[16,64,128]{2,1,0:T(8,128)S(1)}, f32[16,64,128]{2,1,0:T(8,128)S(1)}, u32[]{:S(2)}, u32[]{:S(2)}) collective-permute-start(f32[16,64,128]{2,1,0:T(8,128)S(1)} %collective-permute-done.20.refs_2_), channel_id=1, source_target_pairs={{1,0},{2,1},{3,2},{4,3},{5,4},{6,5},{7,6},{8,7},{9,8},{10,9},{11,1... | collective-permute-start | bytes 1572872 | tf_op jit(solution)/shard_map/ppermute | solution.py:364
  362.1 23.5 %collective-permute-start.11 = (f32[16,64,128]{2,1,0:T(8,128)S(1)}, f32[16,64,128]{2,1,0:T(8,128)S(1)}, u32[]{:S(2)}, u32[]{:S(2)}) collective-permute-start(f32[16,64,128]{2,1,0:T(8,128)S(1)} %collective-permute-done.10.refs_4_), channel_id=1, source_target_pairs={{0,32},{32,64},{64,96},{96,0},{1,33},{33,65},{65,97},{97,1},{2,34}... | collective-permute-start | bytes 1572872 | tf_op jit(solution)/shard_map/ppermute | solution.py:343
  364.3 23.7 %collective-permute-start.19 = (f32[16,64,128]{2,1,0:T(8,128)S(1)}, f32[16,64,128]{2,1,0:T(8,128)S(1)}, u32[]{:S(2)}, u32[]{:S(2)}) collective-permute-start(f32[16,64,128]{2,1,0:T(8,128)S(1)} %collective-permute-done.18.refs_3_), channel_id=1, source_target_pairs={{0,96},{32,0},{64,32},{96,64},{1,97},{33,1},{65,33},{97,65},{2,98}... | collective-permute-start | bytes 1572872 | tf_op jit(solution)/shard_map/ppermute | solution.py:347
  365.5 30.5 %collective-permute-start.26 = (f32[16,64,128]{2,1,0:T(8,128)S(1)}, f32[16,64,128]{2,1,0:T(8,128)S(1)}, u32[]{:S(2)}, u32[]{:S(2)}) collective-permute-start(f32[16,64,128]{2,1,0:T(8,128)S(1)} %collective-permute-done.10.refs_4_), channel_id=1, source_target_pairs={{0,1},{1,2},{2,3},{3,4},{4,5},{5,6},{6,7},{7,8},{8,9},{9,10},{10,1... | collective-permute-start | bytes 1572872 | tf_op jit(solution)/shard_map/ppermute | solution.py:364
  374.4 21.6 %collective-permute-start.25 = (f32[16,64,128]{2,1,0:T(8,128)S(1)}, f32[16,64,128]{2,1,0:T(8,128)S(1)}, u32[]{:S(2)}, u32[]{:S(2)}) collective-permute-start(f32[16,64,128]{2,1,0:T(8,128)S(1)} %collective-permute-done.18.refs_3_), channel_id=1, source_target_pairs={{1,0},{2,1},{3,2},{4,3},{5,4},{6,5},{7,6},{8,7},{9,8},{10,9},{11,1... | collective-permute-start | bytes 1572872 | tf_op jit(solution)/shard_map/ppermute | solution.py:364
  377.0 19.1 %collective-permute-start.27 = (f32[16,64,128]{2,1,0:T(8,128)S(1)}, f32[16,64,128]{2,1,0:T(8,128)S(1)}, u32[]{:S(2)}, u32[]{:S(2)}) collective-permute-start(f32[16,64,128]{2,1,0:T(8,128)S(1)} %collective-permute-done.21.refs_5_), channel_id=1, source_target_pairs={{0,1},{1,2},{2,3},{3,4},{4,5},{5,6},{6,7},{7,8},{8,9},{9,10},{10,1... | collective-permute-start | bytes 1572872 | tf_op jit(solution)/shard_map/ppermute | solution.py:364
  385.6 10.6 %collective-permute-start.22 = (f32[16,64,128]{2,1,0:T(8,128)S(1)}, f32[16,64,128]{2,1,0:T(8,128)}, u32[]{:S(2)}, u32[]{:S(2)}) collective-permute-start(f32[16,64,128]{2,1,0:T(8,128)S(1)} %collective-permute-done.11.refs_0_), channel_id=1, source_target_pairs={{0,1},{1,2},{2,3},{3,4},{4,5},{5,6},{6,7},{7,8},{8,9},{9,10},{10,1... | collective-permute-start | bytes 1572872 | tf_op jit(solution)/shard_map/ppermute | solution.py:364
  388.1 13.8 %collective-permute-start.23 = (f32[16,64,128]{2,1,0:T(8,128)S(1)}, f32[16,64,128]{2,1,0:T(8,128)}, u32[]{:S(2)}, u32[]{:S(2)}) collective-permute-start(f32[16,64,128]{2,1,0:T(8,128)S(1)} %collective-permute-done.19.refs_1_), channel_id=1, source_target_pairs={{0,1},{1,2},{2,3},{3,4},{4,5},{5,6},{6,7},{7,8},{8,9},{9,10},{10,1... | collective-permute-start | bytes 1572872 | tf_op jit(solution)/shard_map/ppermute | solution.py:364
  448.9 20.8 %collective-permute-start.42 = (f32[16,64,128]{2,1,0:T(8,128)S(1)}, f32[16,64,128]{2,1,0:T(8,128)S(1)}, u32[]{:S(2)}, u32[]{:S(2)}) collective-permute-start(f32[16,64,128]{2,1,0:T(8,128)S(1)} %get-tuple-element.75), channel_id=1, source_target_pairs={{0,32},{32,64},{64,96},{96,0},{1,33},{33,65},{65,97},{97,1},{2,34}... | collective-permute-start | bytes 1572872 | tf_op jit(solution)/shard_map/ppermute | solution.py:343
  448.9 24.2 %collective-permute-start.48 = (f32[16,64,128]{2,1,0:T(8,128)S(1)}, f32[16,64,128]{2,1,0:T(8,128)S(1)}, u32[]{:S(2)}, u32[]{:S(2)}) collective-permute-start(f32[16,64,128]{2,1,0:T(8,128)S(1)} %get-tuple-element.80), channel_id=1, source_target_pairs={{0,96},{32,0},{64,32},{96,64},{1,97},{33,1},{65,33},{97,65},{2,98}... | collective-permute-start | bytes 1572872 | tf_op jit(solution)/shard_map/ppermute | solution.py:347
  457.3 12.2 %collective-permute-start.54 = (f32[8,64,128]{2,1,0:T(8,128)S(1)}, f32[8,64,128]{2,1,0:T(8,128)S(1)}, u32[]{:S(2)}, u32[]{:S(2)}) collective-permute-start(f32[8,64,128]{2,1,0:T(8,128)S(1)} %get-tuple-element.83), channel_id=1, source_target_pairs={{0,32},{32,64},{64,96},{96,0},{1,33},{33,65},{65,97},{97,1},{2,34}... | collective-permute-start | bytes 786440 | tf_op jit(solution)/shard_map/ppermute | solution.py:343
  457.4 15.5 %collective-permute-start.60 = (f32[8,64,128]{2,1,0:T(8,128)S(1)}, f32[8,64,128]{2,1,0:T(8,128)S(1)}, u32[]{:S(2)}, u32[]{:S(2)}) collective-permute-start(f32[8,64,128]{2,1,0:T(8,128)S(1)} %get-tuple-element.88), channel_id=1, source_target_pairs={{0,96},{32,0},{64,32},{96,64},{1,97},{33,1},{65,33},{97,65},{2,98}... | collective-permute-start | bytes 786440 | tf_op jit(solution)/shard_map/ppermute | solution.py:347
  460.6 14.6 %collective-permute-start.56 = (f32[8,64,128]{2,1,0:T(8,128)S(1)}, f32[8,64,128]{2,1,0:T(8,128)S(1)}, u32[]{:S(2)}, u32[]{:S(2)}) collective-permute-start(f32[8,64,128]{2,1,0:T(8,128)S(1)} %get-tuple-element.84), channel_id=1, source_target_pairs={{0,96},{32,0},{64,32},{96,64},{1,97},{33,1},{65,33},{97,65},{2,98}... | collective-permute-start | bytes 786440 | tf_op jit(solution)/shard_map/ppermute | solution.py:347
  469.5 10.5 %collective-permute-start.55 = (f32[8,64,128]{2,1,0:T(8,128)S(1)}, f32[8,64,128]{2,1,0:T(8,128)S(1)}, u32[]{:S(2)}, u32[]{:S(2)}) collective-permute-start(f32[8,64,128]{2,1,0:T(8,128)S(1)} %add.142), channel_id=1, source_target_pairs={{0,32},{32,64},{64,96},{96,0},{1,33},{33,65},{65,97},{97,1},{2,34}... | collective-permute-start | bytes 786440 | tf_op jit(solution)/shard_map/ppermute | solution.py:343
  469.6 16.8 %collective-permute-start.44 = (f32[16,64,128]{2,1,0:T(8,128)S(1)}, f32[16,64,128]{2,1,0:T(8,128)S(1)}, u32[]{:S(2)}, u32[]{:S(2)}) collective-permute-start(f32[16,64,128]{2,1,0:T(8,128)S(1)} %get-tuple-element.76), channel_id=1, source_target_pairs={{0,96},{32,0},{64,32},{96,64},{1,97},{33,1},{65,33},{97,65},{2,98}... | collective-permute-start | bytes 1572872 | tf_op jit(solution)/shard_map/ppermute | solution.py:347
  472.9 18.3 %collective-permute-start.43 = (f32[16,64,128]{2,1,0:T(8,128)S(1)}, f32[16,64,128]{2,1,0:T(8,128)S(1)}, u32[]{:S(2)}, u32[]{:S(2)}) collective-permute-start(f32[16,64,128]{2,1,0:T(8,128)S(1)} %add.136), channel_id=1, source_target_pairs={{0,32},{32,64},{64,96},{96,0},{1,33},{33,65},{65,97},{97,1},{2,34}... | collective-permute-start | bytes 1572872 | tf_op jit(solution)/shard_map/ppermute | solution.py:343
  473.1 35.1 %collective-permute-start.59 = (f32[8,64,128]{2,1,0:T(8,128)S(1)}, f32[8,64,128]{2,1,0:T(8,128)S(1)}, u32[]{:S(2)}, u32[]{:S(2)}) collective-permute-start(f32[8,64,128]{2,1,0:T(8,128)S(1)} %get-tuple-element.86), channel_id=1, source_target_pairs={{0,32},{32,64},{64,96},{96,0},{1,33},{33,65},{65,97},{97,1},{2,34}... | collective-permute-start | bytes 786440 | tf_op jit(solution)/shard_map/ppermute | solution.py:343
  475.2 32.7 %collective-permute-start.47 = (f32[16,64,128]{2,1,0:T(8,128)S(1)}, f32[16,64,128]{2,1,0:T(8,128)S(1)}, u32[]{:S(2)}, u32[]{:S(2)}) collective-permute-start(f32[16,64,128]{2,1,0:T(8,128)S(1)} %get-tuple-element.78), channel_id=1, source_target_pairs={{0,32},{32,64},{64,96},{96,0},{1,33},{33,65},{65,97},{97,1},{2,34}... | collective-permute-start | bytes 1572872 | tf_op jit(solution)/shard_map/ppermute | solution.py:343
  480.0 27.9 %collective-permute-start.49 = (f32[16,64,128]{2,1,0:T(8,128)S(1)}, f32[16,64,128]{2,1,0:T(8,128)S(1)}, u32[]{:S(2)}, u32[]{:S(2)}) collective-permute-start(f32[16,64,128]{2,1,0:T(8,128)S(1)} %add.140), channel_id=1, source_target_pairs={{0,96},{32,0},{64,32},{96,64},{1,97},{33,1},{65,33},{97,65},{2,98}... | collective-permute-start | bytes 1572872 | tf_op jit(solution)/shard_map/ppermute | solution.py:347
  486.5 25.1 %collective-permute-start.61 = (f32[8,64,128]{2,1,0:T(8,128)S(1)}, f32[8,64,128]{2,1,0:T(8,128)S(1)}, u32[]{:S(2)}, u32[]{:S(2)}) collective-permute-start(f32[8,64,128]{2,1,0:T(8,128)S(1)} %add.146), channel_id=1, source_target_pairs={{0,96},{32,0},{64,32},{96,64},{1,97},{33,1},{65,33},{97,65},{2,98}... | collective-permute-start | bytes 786440 | tf_op jit(solution)/shard_map/ppermute | solution.py:347
  491.2 20.5 %collective-permute-start.64 = (f32[8,64,128]{2,1,0:T(8,128)S(1)}, f32[8,64,128]{2,1,0:T(8,128)S(1)}, u32[]{:S(2)}, u32[]{:S(2)}) collective-permute-start(f32[8,64,128]{2,1,0:T(8,128)S(1)} %multiply_divide_fusion.5.refs_14_), channel_id=1, source_target_pairs={{0,96},{32,0},{64,32},{96,64},{1,97},{33,1},{65,33},{97,65},{2,98}... | collective-permute-start | bytes 786440 | tf_op jit(solution)/shard_map/ppermute | solution.py:347
  507.9 10.4 %collective-permute-start.57 = (f32[8,64,128]{2,1,0:T(8,128)S(1)}, f32[8,64,128]{2,1,0:T(8,128)S(1)}, u32[]{:S(2)}, u32[]{:S(2)}) collective-permute-start(f32[8,64,128]{2,1,0:T(8,128)S(1)} %multiply_divide_fusion.5.refs_14_), channel_id=1, source_target_pairs={{0,32},{32,64},{64,96},{96,0},{1,33},{33,65},{65,97},{97,1},{2,34}... | collective-permute-start | bytes 786440 | tf_op jit(solution)/shard_map/ppermute | solution.py:343
  507.9 29.3 %collective-permute-start.45 = (f32[16,64,128]{2,1,0:T(8,128)S(1)}, f32[16,64,128]{2,1,0:T(8,128)S(1)}, u32[]{:S(2)}, u32[]{:S(2)}) collective-permute-start(f32[16,64,128]{2,1,0:T(8,128)S(1)} %multiply_divide_fusion.1.refs_6_), channel_id=1, source_target_pairs={{0,32},{32,64},{64,96},{96,0},{1,33},{33,65},{65,97},{97,1},{2,34}... | collective-permute-start | bytes 1572872 | tf_op jit(solution)/shard_map/ppermute | solution.py:343
  508.2 29.1 %collective-permute-start.50 = (f32[16,64,128]{2,1,0:T(8,128)S(1)}, f32[16,64,128]{2,1,0:T(8,128)S(1)}, u32[]{:S(2)}, u32[]{:S(2)}) collective-permute-start(f32[16,64,128]{2,1,0:T(8,128)S(1)} %multiply_divide_fusion.refs_7_), channel_id=1, source_target_pairs={{0,96},{32,0},{64,32},{96,64},{1,97},{33,1},{65,33},{97,65},{2,98}... | collective-permute-start | bytes 1572872 | tf_op jit(solution)/shard_map/ppermute | solution.py:347
  511.6 23.6 %collective-permute-start.65 = (f32[8,64,128]{2,1,0:T(8,128)S(1)}, f32[8,64,128]{2,1,0:T(8,128)S(1)}, u32[]{:S(2)}, u32[]{:S(2)}) collective-permute-start(f32[8,64,128]{2,1,0:T(8,128)S(1)} %multiply_divide_fusion.4.refs_15_), channel_id=1, source_target_pairs={{0,32},{32,64},{64,96},{96,0},{1,33},{33,65},{65,97},{97,1},{2,34}... | collective-permute-start | bytes 786440 | tf_op jit(solution)/shard_map/ppermute | solution.py:343
  511.7 23.5 %collective-permute-start.62 = (f32[8,64,128]{2,1,0:T(8,128)S(1)}, f32[8,64,128]{2,1,0:T(8,128)S(1)}, u32[]{:S(2)}, u32[]{:S(2)}) collective-permute-start(f32[8,64,128]{2,1,0:T(8,128)S(1)} %multiply_divide_fusion.4.refs_15_), channel_id=1, source_target_pairs={{0,96},{32,0},{64,32},{96,64},{1,97},{33,1},{65,33},{97,65},{2,98}... | collective-permute-start | bytes 786440 | tf_op jit(solution)/shard_map/ppermute | solution.py:347
  518.3 22.5 %collective-permute-start.58 = (f32[8,64,128]{2,1,0:T(8,128)S(1)}, f32[8,64,128]{2,1,0:T(8,128)S(1)}, u32[]{:S(2)}, u32[]{:S(2)}) collective-permute-start(f32[8,64,128]{2,1,0:T(8,128)S(1)} %collective-permute-done.57.refs_12_), channel_id=1, source_target_pairs={{0,32},{32,64},{64,96},{96,0},{1,33},{33,65},{65,97},{97,1},{2,34}... | collective-permute-start | bytes 786440 | tf_op jit(solution)/shard_map/ppermute | solution.py:343
  535.2 28.8 %collective-permute-start.52 = (f32[16,64,128]{2,1,0:T(8,128)S(1)}, f32[16,64,128]{2,1,0:T(8,128)S(1)}, u32[]{:S(2)}, u32[]{:S(2)}) collective-permute-start(f32[16,64,128]{2,1,0:T(8,128)S(1)} %multiply_divide_fusion.1.refs_6_), channel_id=1, source_target_pairs={{0,96},{32,0},{64,32},{96,64},{1,97},{33,1},{65,33},{97,65},{2,98}... | collective-permute-start | bytes 1572872 | tf_op jit(solution)/shard_map/ppermute | solution.py:347
  535.2 28.7 %collective-permute-start.53 = (f32[16,64,128]{2,1,0:T(8,128)S(1)}, f32[16,64,128]{2,1,0:T(8,128)S(1)}, u32[]{:S(2)}, u32[]{:S(2)}) collective-permute-start(f32[16,64,128]{2,1,0:T(8,128)S(1)} %multiply_divide_fusion.refs_7_), channel_id=1, source_target_pairs={{0,32},{32,64},{64,96},{96,0},{1,33},{33,65},{65,97},{97,1},{2,34}... | collective-permute-start | bytes 1572872 | tf_op jit(solution)/shard_map/ppermute | solution.py:343
  537.2 26.7 %collective-permute-start.46 = (f32[16,64,128]{2,1,0:T(8,128)S(1)}, f32[16,64,128]{2,1,0:T(8,128)S(1)}, u32[]{:S(2)}, u32[]{:S(2)}) collective-permute-start(f32[16,64,128]{2,1,0:T(8,128)S(1)} %collective-permute-done.45.refs_4_), channel_id=1, source_target_pairs={{0,32},{32,64},{64,96},{96,0},{1,33},{33,65},{65,97},{97,1},{2,34}... | collective-permute-start | bytes 1572872 | tf_op jit(solution)/shard_map/ppermute | solution.py:343
  537.3 26.7 %collective-permute-start.51 = (f32[16,64,128]{2,1,0:T(8,128)S(1)}, f32[16,64,128]{2,1,0:T(8,128)S(1)}, u32[]{:S(2)}, u32[]{:S(2)}) collective-permute-start(f32[16,64,128]{2,1,0:T(8,128)S(1)} %collective-permute-done.50.refs_3_), channel_id=1, source_target_pairs={{0,96},{32,0},{64,32},{96,64},{1,97},{33,1},{65,33},{97,65},{2,98}... | collective-permute-start | bytes 1572872 | tf_op jit(solution)/shard_map/ppermute | solution.py:347
  540.8 23.1 %collective-permute-start.63 = (f32[8,64,128]{2,1,0:T(8,128)S(1)}, f32[8,64,128]{2,1,0:T(8,128)S(1)}, u32[]{:S(2)}, u32[]{:S(2)}) collective-permute-start(f32[8,64,128]{2,1,0:T(8,128)S(1)} %collective-permute-done.62.refs_11_), channel_id=1, source_target_pairs={{0,96},{32,0},{64,32},{96,64},{1,97},{33,1},{65,33},{97,65},{2,98}... | collective-permute-start | bytes 786440 | tf_op jit(solution)/shard_map/ppermute | solution.py:347
  (27 other events, 628.5 us)
